TPU v7x, 32 devices: a whole 2x2x4 slice. The times are simulated.
32 devices in a mesh: pipe: 2 (over y), dp: 4 (over z), tensor: 4 (over x, core).
Axes of the slice: x: 2, y: 2, z: 4, core: 2. Of those that a mesh axis runs over, the one named last changes fastest.
Arguments:
- tokens: bfloat16 [3072, 8192], P(('pipe', 'dp'), 'tensor'), parts along dimension 0, may hold values from -6 to 6
- pattern: int32 [128, 6], P('pipe'), parts along dimension 0, may hold values from 0 to 31, as said below
- blocks: bfloat16 [128, 6, 256, 256], P(('pipe', 'tensor'), None, 'dp'), parts along dimension 0, may hold values from -0.15625 to 0.15625
- left_factor: bfloat16 [16384, 512], P(('pipe', 'tensor'), 'dp'), parts along dimension 0, may hold values from -0.0625 to 0.0625
- right_factor: bfloat16 [1024, 16384], P(('pipe', 'dp'), 'tensor'), parts along dimension 0, may hold values from -0.25 to 0.25
- cotangent: bfloat16 [3072, 16384], P(('pipe', 'dp'), 'tensor'), parts along dimension 0, may hold values from -6 to 6
Outputs:
- hidden: bfloat16 [3072, 16384], P(('pipe', 'dp'), 'tensor'), parts along dimension 0
- token_grad: float32 [3072, 8192], P(('pipe', 'dp'), 'tensor'), parts along dimension 0
- block_grad: float32 [128, 6, 256, 256], P(('pipe', 'tensor'), None, 'dp'), parts along dimension 0
- left_grad: float32 [16384, 512], P(('pipe', 'tensor'), 'dp'), parts along dimension 0
- right_grad: float32 [1024, 16384], P(('pipe', 'dp'), 'tensor'), parts along dimension 0
There are 2 independent parts, one for each index of `pipe`. A program takes and returns all parts, laid end to end along the dimension named above; each array names one. Nothing has to cross between parts.
Inputs may be any that keep to these rules, and one draw needn't show every extreme that they name: `pattern`: row j lists the 6 input blocks feeding hidden block j: under a relabeling of the 32 input blocks drawn from the seed, they are the labels of (j mod 32) XOR s for s = 0 and then the powers of two below 32 in rising order; a row's entries are distinct.
All inputs are finite; a program needn't handle non-finite values.
Results may differ from a plain program's by a relative error of at most 0.017.
Values may be sent and summed in bfloat16 or wider, within the bound.
A program may use at most 256 MiB of HBM per device.

v0:
```python
import jax
import jax.numpy as jnp
from jax import lax
from jax.sharding import PartitionSpec as P

SQRT_HALF = 0.7071067811865476
INV_ROOT_TWO_PI = 0.3989422804014327


def gelu_parts(preact):
    normal_cdf = 0.5 * (1.0 + jax.scipy.special.erf(preact * SQRT_HALF))
    return (
        preact * normal_cdf,
        normal_cdf + preact * jnp.exp(-0.5 * preact * preact) * INV_ROOT_TWO_PI,
    )


def per_device(tokens, pattern, blocks, left_factor, right_factor, cotangent):
    tok_rows = tokens.shape[0]
    block_size = blocks.shape[3]
    local_cols = blocks.shape[0]
    slot_count = blocks.shape[1]
    full_tokens = lax.all_gather(tokens, "tensor", axis=1, tiled=True)
    block_count = full_tokens.shape[1] // block_size
    tensor_rank = lax.axis_index("tensor")
    local_pattern = lax.dynamic_slice_in_dim(pattern, tensor_rank * local_cols, local_cols, 0)
    picked = jnp.take(full_tokens.reshape(tok_rows, block_count, block_size), local_pattern, axis=1)
    inputs = picked
    butterfly = jnp.einsum(
        "tjkc,jkcd->tjd",
        inputs,
        lax.all_gather(blocks, "dp", axis=2, tiled=True),
        preferred_element_type=jnp.float32,
    )
    left_rows = lax.all_gather(left_factor, "dp", axis=1, tiled=True)
    whole_left = lax.all_gather(left_rows, "tensor", axis=0, tiled=True)
    rank_acts = jnp.dot(full_tokens, whole_left, preferred_element_type=jnp.float32).astype(
        jnp.bfloat16
    )
    inputs = rank_acts
    rank_part = jnp.dot(
        inputs,
        lax.all_gather(right_factor, "dp", axis=0, tiled=True),
        preferred_element_type=jnp.float32,
    )
    preact = butterfly.reshape(tok_rows, -1) + rank_part
    activated, slope_values = gelu_parts(preact)
    hidden = activated.astype(jnp.bfloat16)
    grad_pre = (cotangent.astype(jnp.float32) * slope_values).astype(jnp.bfloat16)
    rank_terms = lax.dot_general(
        grad_pre,
        lax.all_gather(right_factor, "dp", axis=0, tiled=True),
        (((1,), (1,)), ((), ())),
        preferred_element_type=jnp.float32,
    )
    rank_grad = lax.psum(rank_terms.astype(jnp.bfloat16), "tensor")
    right_term = lax.dot_general(
        rank_acts, grad_pre, (((0,), (0,)), ((), ())), preferred_element_type=jnp.float32
    )
    right_grad = lax.psum_scatter(
        right_term.astype(jnp.bfloat16), "dp", scatter_dimension=0, tiled=True
    ).astype(jnp.float32)
    left_term = lax.dot_general(
        tokens, rank_grad, (((0,), (0,)), ((), ())), preferred_element_type=jnp.float32
    )
    left_grad = lax.psum_scatter(
        left_term.astype(jnp.bfloat16), "dp", scatter_dimension=1, tiled=True
    ).astype(jnp.float32)
    grad_blocks = grad_pre.reshape(tok_rows, local_cols, block_size)
    block_term = jnp.einsum(
        "tjkc,tjd->jkcd", picked, grad_blocks, preferred_element_type=jnp.float32
    )
    block_grad = lax.psum_scatter(
        block_term.astype(jnp.bfloat16), "dp", scatter_dimension=2, tiled=True
    ).astype(jnp.float32)
    spread = jnp.einsum(
        "tjd,jkcd->tjkc",
        grad_blocks,
        lax.all_gather(blocks, "dp", axis=2, tiled=True),
        preferred_element_type=jnp.float32,
    )
    placed = (
        jnp.zeros((tok_rows, block_count, block_size), jnp.float32)
        .at[:, local_pattern.reshape(-1)]
        .add(spread.reshape(tok_rows, local_cols * slot_count, block_size))
    )
    token_part = lax.psum_scatter(
        placed.reshape(tok_rows, -1).astype(jnp.bfloat16), "tensor", scatter_dimension=1, tiled=True
    ).astype(jnp.float32)
    token_grad = token_part + lax.dot_general(
        rank_grad, left_rows, (((1,), (1,)), ((), ())), preferred_element_type=jnp.float32
    )
    return (hidden, token_grad, block_grad, left_grad, right_grad)


def solution(mesh):
    placed = (
        P(("pipe", "dp"), "tensor"),
        P("pipe", None),
        P(("pipe", "tensor"), None, "dp", None),
        P(("pipe", "tensor"), "dp"),
        P(("pipe", "dp"), "tensor"),
        P(("pipe", "dp"), "tensor"),
    )
    return jax.shard_map(
        per_device,
        mesh=mesh,
        in_specs=placed,
        out_specs=(
            P(("pipe", "dp"), "tensor"),
            P(("pipe", "dp"), "tensor"),
            P(("pipe", "tensor"), None, "dp", None),
            P(("pipe", "tensor"), "dp"),
            P(("pipe", "dp"), "tensor"),
        ),
        check_vma=False,
    )
```

profile of v0, /device:TPU:0, one launch (start us, length us, event | category | flops | bytes accessed | tf_op | source)
XLA Modules:
  0.0 936.8 jit_solution(5141369474184893608)
XLA Ops:
  7.2 0.7 all-gather.10.cloned.1.call-update
  8.0 2.6 copy.32
  10.6 47.9 %all-gather.10.cloned.1.call-done = bf16[2048,512]{1,0:T(8,128)(2,1)} async-done(((bf16[2048,128]{1,0:T(8,128)(2,1)}), bf16[2048,512]{1,0:T(8,128)(2,1)}) %all-gather.10.cloned.1.call-update) | async-done | bytes 2097168 | tf_op jit(solution)/shard_map/all_gather | solution.py:35
  60.2 45.2 %all-gather.6.cloned.1.call-done = bf16[384,8192]{0,1:T(8,128)(2,1)} async-done(((bf16[384,2048]{0,1:T(8,128)(2,1)}), bf16[384,8192]{0,1:T(8,128)(2,1)}) %all-gather.6.cloned.1.call-update) | async-done | bytes 6291472 | tf_op jit(solution)/shard_map/all_gather | solution.py:23
  105.3 8.6 copy.34
  114.0 13.0 %gather_fusion = bf16[96,384,256]{2,1,0:T(8,128)(2,1)} fusion(bf16[384,32,256]{2,0,1:T(8,128)(2,1)} %copy.34, s32[1024]{0:T(1024)S(1)} %pad_clamp_fusion), kind=kCustom, calls=%fused_computation | custom fusion | bytes 37749120 | tf_op jit(solution)/shard_map/jit(_take)/gather | solution.py:27
  126.9 24.7 %copy.35 = bf16[16,6,384,256]{2,3,1,0:T(8,128)(2,1)} copy(bf16[16,6,384,256]{3,2,1,0:T(8,128)(2,1)} %bitcast.47) | data formatting | bytes 37748736 | tf_op jit(solution)/shard_map/jit(_take)/gather | solution.py:27
  151.6 13.6 %all-gather.12.cloned.1.call-done = bf16[8192,512]{1,0:T(8,128)(2,1)} async-done(((bf16[2048,512]{1,0:T(8,128)(2,1)}), bf16[8192,512]{1,0:T(8,128)(2,1)}) %all-gather.12.cloned.1.call-update) | async-done | bytes 8388624 | tf_op jit(solution)/shard_map/all_gather | solution.py:36
  165.2 8.6 convolution_convert_fusion.3
  173.8 211.0 %all-gather.8.cloned.1.call-done = bf16[16,6,256,256]{3,2,1,0:T(8,128)(2,1)} async-done(((bf16[16,6,64,256]{3,2,1,0:T(8,128)(2,1)}), bf16[16,6,256,256]{3,2,1,0:T(8,128)(2,1)}) %all-gather.8.cloned.1.call-update) | async-done | bytes 12582928 | tf_op jit(solution)/shard_map/all_gather | solution.py:32
  384.9 16.6 %fusion.2 = f32[16,384,256,1]{1,2,3,0:T(8,128)} fusion(bf16[16,6,256,256]{3,2,1,0:T(8,128)(2,1)} %all-gather.8.cloned.1.call-done, bf16[16,6,384,256]{2,3,1,0:T(8,128)(2,1)} %copy.35, pred[16,6]{1,0:T(8,128)(4,1)S(1)} %copy.31), kind=kOutput, calls=%fused_computation.4 | convolution fusion | flops 4841275392 | bytes 37748832 | tf_op jit(solution)/shard_map/tjkc,jkcd->tjd/dot_general | solution.py:29
  401.5 6.6 copy.37
  408.1 57.2 %all-gather.14.cloned.1.call-done = bf16[512,4096]{1,0:T(8,128)(2,1)} async-done(((bf16[128,4096]{1,0:T(8,128)(2,1)}), bf16[512,4096]{1,0:T(8,128)(2,1)}) %all-gather.14.cloned.1.call-update) | async-done | bytes 4194320 | tf_op jit(solution)/shard_map/all_gather | solution.py:43
  465.3 10.5 %fusion.14 = (bf16[384,4096]{1,0:T(8,128)(2,1)S(1)}, bf16[384,4096]{1,0:T(8,128)(2,1)}) fusion(bf16[384,4096]{1,0:T(8,128)(2,1)} %param.11, f32[384,4096]{1,0:T(8,128)} %copy.37, bf16[384,512]{1,0:T(8,128)(2,1)S(1)} %convolution_convert_fusion.3, bf16[512,4096]{1,0:T(8,128)(2,1)} %all-gather.14.cloned.1.call-done), kind=kOutput, calls=%fused_computation.16 | convolution fusion | flops 1632632832 | bytes 20316160 | tf_op jit(solution)/shard_map/dot_general | solution.py:41
  475.8 2.6 convolution_convert_fusion.2
  478.7 31.1 %all-reduce.2.cloned.1.call-done = bf16[384,512]{1,0:T(8,128)(2,1)} async-done(((bf16[384,512]{1,0:T(8,128)(2,1)}), bf16[384,512]{1,0:T(8,128)(2,1)}) %all-reduce.2.cloned.1.call-update) | async-done | bytes 393232 | tf_op jit(solution)/shard_map/psum | solution.py:56
  509.8 4.1 fusion.18
  514.0 4.4 convolution_convert_fusion
  518.7 3.3 copy.52
  522.0 25.2 %fusion.16 = f32[16,384,6,256]{3,1,2,0:T(8,128)} fusion(bf16[16,6,256,256]{3,2,1,0:T(8,128)(2,1)} %all-gather.8.cloned.1.call-done, bf16[384,16,256,1]{2,1,0,3:T(8,128)(2,1)S(1)} %bitcast.50), kind=kOutput, calls=%fused_computation.25 | convolution fusion | flops 4831838208 | bytes 53477376 | tf_op jit(solution)/shard_map/tjd,jkcd->tjkc/dot_general | solution.py:76
  547.2 5.9 broadcast_in_dim.19
  553.1 90.2 %scatter_fusion = f32[384,32,256]{2,0,1:T(8,128)} fusion(f32[384,32,256]{2,0,1:T(8,128)} %broadcast_in_dim.19, s32[96]{0:T(128)S(1)} %fusion.19, f32[96,384,256]{2,1,0:T(8,128)} %bitcast.46), kind=kCustom, calls=%fused_computation.1 | custom fusion | flops 9437184 | bytes 113246592 | tf_op jit(solution)/shard_map/scatter-add | solution.py:85
  643.3 5.4 convert_bitcast_fusion
  648.8 3.5 copy.51
  652.6 1.6 copy-done.1
  654.2 15.2 %fusion.6 = bf16[16,6,256,256]{3,2,1,0:T(8,128)(2,1)} fusion(bf16[16,6,384,256]{2,3,1,0:T(8,128)(2,1)} %copy.35, pred[16,6]{1,0:T(8,128)(4,1)S(1)} %copy.31, bf16[384,16,256,1]{2,1,0,3:T(8,128)(2,1)S(1)} %bitcast.51), kind=kOutput, calls=%fused_computation.10 | convolution fusion | flops 4847566848 | bytes 34603104 | tf_op jit(solution)/shard_map/tjkc,tjd->jkcd/dot_general | solution.py:70
  669.5 2.4 copy.42
  671.9 2.9 convert_element_type.59
  674.8 35.7 %reduce-scatter.5.cloned.1.call-done = bf16[384,2048]{1,0:T(8,128)(2,1)} async-done(((bf16[384,8192]{1,0:T(8,128)(2,1)}), bf16[384,2048]{1,0:T(8,128)(2,1)}) %reduce-scatter.5.cloned.1.call-update) | async-done | bytes 1572880 | tf_op jit(solution)/shard_map/reduce_scatter | solution.py:87
  710.4 4.1 convert_add_fusion
  714.5 210.0 %reduce-scatter.7.cloned.1.call-done = bf16[16,6,64,256]{3,2,1,0:T(8,128)(2,1)} async-done(((bf16[16,6,256,256]{3,2,1,0:T(8,128)(2,1)}), bf16[16,6,64,256]{3,2,1,0:T(8,128)(2,1)}) %reduce-scatter.7.cloned.1.call-update) | async-done | bytes 3145744 | tf_op jit(solution)/shard_map/reduce_scatter | solution.py:73
  924.5 5.5 convert_element_type.54
  (43 shorter events, 2.6 us)
Async XLA Ops:
  7.2 52.6 %copy-start.5 = (s32[64,6]{0,1:T(8,128)S(1)}, s32[64,6]{0,1:T(8,128)}, u32[]{:S(2)}) copy-start(s32[64,6]{0,1:T(8,128)} %param.7) | copy-start | bytes 4612
  7.2 51.4 %all-gather.10.cloned.1.call-start = ((), (), s32[]{:S(2)}) async-start(), calls=%async_computation.6 | async-start | bytes 2621440 | tf_op jit(solution)/shard_map/all_gather | solution.py:35
  7.9 97.4 %all-gather.6.cloned.1.call-start = ((), (), s32[]{:S(2)}) async-start(), calls=%async_computation.4 | async-start | bytes 7864320 | tf_op jit(solution)/shard_map/all_gather | solution.py:23
  10.6 154.6 %all-gather.12.cloned.1.call-start = ((), (), s32[]{:S(2)}) async-start(), calls=%async_computation.7 | async-start | bytes 10485760 | tf_op jit(solution)/shard_map/all_gather | solution.py:36
  58.6 326.3 %all-gather.8.cloned.1.call-start = ((), (), s32[]{:S(2)}) async-start(), calls=%async_computation.5 | async-start | bytes 15728640 | tf_op jit(solution)/shard_map/all_gather | solution.py:32
  59.1 406.1 %all-gather.14.cloned.1.call-start = ((), (), s32[]{:S(2)}) async-start(), calls=%async_computation.8 | async-start | bytes 5242880 | tf_op jit(solution)/shard_map/all_gather | solution.py:43
  59.7 450.0 %all-reduce.2.cloned.1.call-start = ((), (), s32[]{:S(2)}) async-start(), calls=%async_computation.10 | async-start | bytes 786432 | tf_op jit(solution)/shard_map/psum | solution.py:56
  465.3 10.5 %copy-start.6 = (bf16[512,4096]{1,0:T(8,128)(2,1)S(1)}, bf16[512,4096]{1,0:T(8,128)(2,1)}, u32[]{:S(2)}) copy-start(bf16[512,4096]{1,0:T(8,128)(2,1)} %all-gather.14.cloned.1.call-done) | copy-start | bytes 12582916
  475.8 38.2 %copy-start.2 = (bf16[384,4096]{1,0:T(8,128)(2,1)}, bf16[384,4096]{1,0:T(8,128)(2,1)S(1)}, u32[]{:S(2)}) copy-start(bf16[384,4096]{1,0:T(8,128)(2,1)S(1)} %get-tuple-element.22) | copy-start | bytes 9437188
  478.5 191.0 %reduce-scatter.9.cloned.1.call-start = ((), (), s32[]{:S(2)}) async-start(), calls=%async_computation.12 | async-start | bytes 2621440 | tf_op jit(solution)/shard_map/reduce_scatter | solution.py:66
  513.9 157.9 %reduce-scatter.11.cloned.1.call-start = ((), (), s32[]{:S(2)}) async-start(), calls=%async_computation.13 | async-start | bytes 5242880 | tf_op jit(solution)/shard_map/reduce_scatter | solution.py:60
  518.5 192.0 %reduce-scatter.5.cloned.1.call-start = ((), (), s32[]{:S(2)}) async-start(), calls=%async_computation.9 | async-start | bytes 7864320 | tf_op jit(solution)/shard_map/reduce_scatter | solution.py:87
  522.0 25.2 %copy-start = (bf16[48,8,16,256]{3,2,1,0:T(8,128)(2,1)}, bf16[48,8,16,256]{3,2,1,0:T(8,128)(2,1)S(1)}, u32[]{:S(2)}) copy-start(bf16[48,8,16,256]{3,2,1,0:T(8,128)(2,1)S(1)} %copy.52) | copy-start | bytes 9437188
  652.3 1.9 copy-start.1
  652.3 272.2 %reduce-scatter.7.cloned.1.call-start = ((), (), s32[]{:S(2)}) async-start(), calls=%async_computation.11 | async-start | bytes 15728640 | tf_op jit(solution)/shard_map/reduce_scatter | solution.py:73
  669.4 41.0 %copy-start.3 = (bf16[2048,512]{1,0:T(8,128)(2,1)S(1)}, bf16[2048,512]{1,0:T(8,128)(2,1)}, u32[]{:S(2)}) copy-start(bf16[2048,512]{1,0:T(8,128)(2,1)} %all-gather.10.cloned.1.call-done) | copy-start | bytes 6291460
  669.4 41.0 %copy-start.4 = (bf16[384,512]{1,0:T(8,128)(2,1)S(1)}, bf16[384,512]{1,0:T(8,128)(2,1)}, u32[]{:S(2)}) copy-start(bf16[384,512]{1,0:T(8,128)(2,1)} %all-reduce.2.cloned.1.call-done) | copy-start | bytes 1179652
Sparse Core Ops, SparseCore 0:
  9.6 48.9 all-gather.9
  60.7 44.5 all-gather.5
  106.9 58.2 all-gather.11
  166.6 218.2 all-gather.7
  386.3 78.9 all-gather.13
  478.6 31.1 all-reduce.1
  514.0 43.8 reduce-scatter.8
  560.2 76.0 reduce-scatter.10
  652.4 57.9 reduce-scatter.4
  712.6 211.8 reduce-scatter.6
where the time goes:
time: 939 us; the launch traced here: 937 us
  waiting for transfers between devices  654 us (70%)
  other arithmetic  104 us (11%)
  matrix products  91.5 us (10%)
  local copies, waits for them, and re-layouts  72.6 us (8%)
  between operations  14.3 us (2%)
    all_gather x1, waiting for transfers between devices, per_device(): lax.all_gather(blocks, 'dp', axis=2, tiled=True)  211 us
    reduce_scatter x1, waiting for transfers between devices, per_device(): lax.psum_scatter(block_term.astype(jnp.bfloat16), 'dp', scatter_dimension...  210 us
    scatter-add x1, other arithmetic, per_device(): placed = jnp.zeros((tok_rows, block_count, block_size), jnp.float32).at[:...  90.2 us
    all_gather x1, waiting for transfers between devices, per_device(): lax.all_gather(right_factor, 'dp', axis=0, tiled=True)  57.2 us
    all_gather x1, waiting for transfers between devices, per_device(): left_rows = lax.all_gather(left_factor, 'dp', axis=1, tiled=True)  47.9 us
    all_gather x1, waiting for transfers between devices, per_device(): full_tokens = lax.all_gather(tokens, 'tensor', axis=1, tiled=True)  45.2 us
    gather x2, local copies, waits for them, and re-layouts, per_device(): jnp.take(full_tokens.reshape(tok_rows, block_count, block_size), local_pa...  37.6 us
    reduce_scatter x1, waiting for transfers between devices, per_device(): lax.psum_scatter(placed.reshape(tok_rows, -1).astype(jnp.bfloat16), 'tens...  35.7 us
  transfers between devices with their start and end apart: 10, of which 8 were waited for; matrix products, arithmetic and copies ran while one was open for 26% of the time, Pallas kernels for 0%

commit v1 on v0

--- a/solution.py
+++ b/solution.py
@@ -32,7 +32,12 @@
         lax.all_gather(blocks, "dp", axis=2, tiled=True),
         preferred_element_type=jnp.float32,
     )
-    left_rows = lax.all_gather(left_factor, "dp", axis=1, tiled=True)
+    ring = [left_factor]
+    for hop in range(3):
+        ring.append(lax.ppermute(ring[-1], "dp", [(dev, (dev + 1) % 4) for dev in range(4)]))
+    left_rows = jnp.roll(
+        jnp.concatenate(ring[::-1], axis=1), (lax.axis_index("dp") + 1) * ring[0].shape[1], axis=1
+    )
     whole_left = lax.all_gather(left_rows, "tensor", axis=0, tiled=True)
     rank_acts = jnp.dot(full_tokens, whole_left, preferred_element_type=jnp.float32).astype(
         jnp.bfloat16

time: 939 us -> 893 us (0.951)
  waiting for transfers between devices: 654 us -> 601 us
    all_gather x1 -> x0, waiting for transfers between devices: 47.9 us -> none  [per_device(): left_rows = lax.all_gather(left_factor, 'dp', axis=1, tiled=True)]
    all_gather x1, waiting for transfers between devices: 45.2 us -> 0.02 us  [per_device(): full_tokens = lax.all_gather(tokens, 'tensor', axis=1, tiled=True)]
    ppermute x0 -> x3, waiting for transfers between devices: none -> 42.8 us  [per_device(): lax.ppermute(ring[-1], 'dp', [(dev, (dev + 1) % 4) for dev in range(4)])]
  transfers between devices with their start and end apart: 10 -> 12, of which waited for: 8 -> 9; matrix products, arithmetic and copies ran while one was open for 26% -> 28% of each run, Pallas kernels for 0% -> 0%
where the time goes in v1:
time: 893 us; the launch traced here: 891 us
  waiting for transfers between devices  601 us (67%)
  other arithmetic  104 us (12%)
  matrix products  92.1 us (10%)
  local copies, waits for them, and re-layouts  76 us (9%)
  between operations  14 us (2%)
    reduce_scatter x1, waiting for transfers between devices, per_device(): lax.psum_scatter(block_term.astype(jnp.bfloat16), 'dp', scatter_dimension...  210 us
    all_gather x1, waiting for transfers between devices, per_device(): lax.all_gather(blocks, 'dp', axis=2, tiled=True)  210 us
    scatter-add x1, other arithmetic, per_device(): placed = jnp.zeros((tok_rows, block_count, block_size), jnp.float32).at[:...  90.3 us
    all_gather x1, waiting for transfers between devices, per_device(): lax.all_gather(right_factor, 'dp', axis=0, tiled=True)  57.2 us
    ppermute x3, waiting for transfers between devices, per_device(): lax.ppermute(ring[-1], 'dp', [(dev, (dev + 1) % 4) for dev in range(4)])  42.8 us
    gather x2, local copies, waits for them, and re-layouts, per_device(): jnp.take(full_tokens.reshape(tok_rows, block_count, block_size), local_pa...  37.9 us
    reduce_scatter x1, waiting for transfers between devices, per_device(): lax.psum_scatter(placed.reshape(tok_rows, -1).astype(jnp.bfloat16), 'tens...  36.7 us
    psum x1, waiting for transfers between devices, per_device(): rank_grad = lax.psum(rank_terms.astype(jnp.bfloat16), 'tensor')  31 us
  transfers between devices with their start and end apart: 12, of which 9 were waited for; matrix products, arithmetic and copies ran while one was open for 28% of the time, Pallas kernels for 0%

profile of v1, /device:TPU:0, one launch (start us, length us, event | category | flops | bytes accessed | tf_op | source)
XLA Modules:
  0.0 891.3 jit_solution(4519168670593001249)
XLA Ops:
  7.2 2.6 copy.32
  9.9 3.1 collective-permute-start
  13.0 13.9 %collective-permute-done = bf16[2048,128]{1,0:T(8,128)(2,1)S(1)} collective-permute-done((bf16[2048,128]{1,0:T(8,128)(2,1)S(1)}, bf16[2048,128]{1,0:T(8,128)(2,1)S(1)}, u32[]{:S(2)}, u32[]{:S(2)}) %collective-permute-start) | collective-permute-done | bytes 524320 | tf_op jit(solution)/shard_map/ppermute | solution.py:37
  27.0 14.9 %collective-permute-done.1 = bf16[2048,128]{1,0:T(8,128)(2,1)S(1)} collective-permute-done((bf16[2048,128]{1,0:T(8,128)(2,1)S(1)}, bf16[2048,128]{1,0:T(8,128)(2,1)S(1)}, u32[]{:S(2)}, u32[]{:S(2)}) %collective-permute-start.1) | collective-permute-done | bytes 524320 | tf_op jit(solution)/shard_map/ppermute | solution.py:37
  41.9 14.0 %collective-permute-done.2 = bf16[2048,128]{1,0:T(8,128)(2,1)S(1)} collective-permute-done((bf16[2048,128]{1,0:T(8,128)(2,1)S(1)}, bf16[2048,128]{1,0:T(8,128)(2,1)S(1)}, u32[]{:S(2)}, u32[]{:S(2)}) %collective-permute-start.2) | collective-permute-done | bytes 524320 | tf_op jit(solution)/shard_map/ppermute | solution.py:37
  60.9 8.7 copy.34
  69.6 13.3 %gather_fusion = bf16[96,384,256]{2,1,0:T(8,128)(2,1)} fusion(bf16[384,32,256]{2,0,1:T(8,128)(2,1)} %copy.34, s32[1024]{0:T(1024)S(1)} %pad_clamp_fusion), kind=kCustom, calls=%fused_computation | custom fusion | bytes 37749120 | tf_op jit(solution)/shard_map/jit(_take)/gather | solution.py:27
  82.8 24.7 %copy.35 = bf16[16,6,384,256]{2,3,1,0:T(8,128)(2,1)} copy(bf16[16,6,384,256]{3,2,1,0:T(8,128)(2,1)} %bitcast.47) | data formatting | bytes 37748736 | tf_op jit(solution)/shard_map/jit(_take)/gather | solution.py:27
  107.5 11.6 %all-gather.9.cloned.1.call-done = bf16[8192,512]{1,0:T(8,128)(2,1)} async-done(((bf16[2048,512]{1,0:T(8,128)(2,1)}), bf16[8192,512]{1,0:T(8,128)(2,1)}) %all-gather.9.cloned.1.call-update) | async-done | bytes 8388624 | tf_op jit(solution)/shard_map/all_gather | solution.py:41
  119.1 9.7 %convolution_convert_fusion.3 = bf16[512,384]{1,0:T(8,128)(2,1)S(1)} fusion(bf16[8192,512]{1,0:T(8,128)(2,1)} %all-gather.9.cloned.1.call-done, bf16[384,8192]{0,1:T(8,128)(2,1)} %all-gather.5.cloned.1.call-done), kind=kOutput, calls=%fused_computation.29 | convolution fusion | flops 3221422080 | bytes 15073280 | tf_op jit(solution)/shard_map/dot_general | solution.py:42
  128.8 210.1 %all-gather.7.cloned.1.call-done = bf16[16,6,256,256]{3,2,1,0:T(8,128)(2,1)} async-done(((bf16[16,6,64,256]{3,2,1,0:T(8,128)(2,1)}), bf16[16,6,256,256]{3,2,1,0:T(8,128)(2,1)}) %all-gather.7.cloned.1.call-update) | async-done | bytes 12582928 | tf_op jit(solution)/shard_map/all_gather | solution.py:32
  339.0 16.6 %fusion.2 = f32[16,384,256,1]{1,2,3,0:T(8,128)} fusion(bf16[16,6,256,256]{3,2,1,0:T(8,128)(2,1)} %all-gather.7.cloned.1.call-done, bf16[16,6,384,256]{2,3,1,0:T(8,128)(2,1)} %copy.35, pred[16,6]{1,0:T(8,128)(4,1)S(1)} %copy.31), kind=kOutput, calls=%fused_computation.4 | convolution fusion | flops 4841275392 | bytes 37748832 | tf_op jit(solution)/shard_map/tjkc,jkcd->tjd/dot_general | solution.py:29
  355.6 6.6 copy.37
  362.2 57.2 %all-gather.11.cloned.1.call-done = bf16[512,4096]{1,0:T(8,128)(2,1)} async-done(((bf16[128,4096]{1,0:T(8,128)(2,1)}), bf16[512,4096]{1,0:T(8,128)(2,1)}) %all-gather.11.cloned.1.call-update) | async-done | bytes 4194320 | tf_op jit(solution)/shard_map/all_gather | solution.py:48
  419.4 10.5 %fusion.14 = (bf16[384,4096]{1,0:T(8,128)(2,1)S(1)}, bf16[384,4096]{1,0:T(8,128)(2,1)}) fusion(bf16[384,4096]{1,0:T(8,128)(2,1)} %param.11, f32[384,4096]{1,0:T(8,128)} %copy.37, bf16[512,384]{1,0:T(8,128)(2,1)S(1)} %convolution_convert_fusion.3, bf16[512,4096]{1,0:T(8,128)(2,1)} %all-gather.11.cloned.1.call-done), kind=kOutput, calls=%fused_computation.16 | convolution fusion | flops 1632632832 | bytes 20316160 | tf_op jit(solution)/shard_map/dot_general | solution.py:46
  429.9 2.6 convolution_convert_fusion.2
  432.8 31.0 %all-reduce.2.cloned.1.call-done = bf16[384,512]{1,0:T(8,128)(2,1)} async-done(((bf16[384,512]{1,0:T(8,128)(2,1)}), bf16[384,512]{1,0:T(8,128)(2,1)}) %all-reduce.2.cloned.1.call-update) | async-done | bytes 393232 | tf_op jit(solution)/shard_map/psum | solution.py:61
  463.8 4.1 fusion.18
  468.0 4.4 convolution_convert_fusion
  472.7 3.3 copy.52
  476.0 25.3 %fusion.16 = f32[16,384,6,256]{3,1,2,0:T(8,128)} fusion(bf16[16,6,256,256]{3,2,1,0:T(8,128)(2,1)} %all-gather.7.cloned.1.call-done, bf16[384,16,256,1]{2,1,0,3:T(8,128)(2,1)S(1)} %bitcast.49), kind=kOutput, calls=%fused_computation.25 | convolution fusion | flops 4831838208 | bytes 53477376 | tf_op jit(solution)/shard_map/tjd,jkcd->tjkc/dot_general | solution.py:81
  501.3 5.9 broadcast_in_dim.19
  507.3 90.3 %scatter_fusion = f32[384,32,256]{2,0,1:T(8,128)} fusion(f32[384,32,256]{2,0,1:T(8,128)} %broadcast_in_dim.19, s32[96]{0:T(128)S(1)} %fusion.19, f32[96,384,256]{2,1,0:T(8,128)} %bitcast.46), kind=kCustom, calls=%fused_computation.1 | custom fusion | flops 9437184 | bytes 113246592 | tf_op jit(solution)/shard_map/scatter-add | solution.py:90
  597.5 5.4 convert_bitcast_fusion
  602.9 3.5 copy.51
  608.4 14.8 %fusion.6 = bf16[16,6,256,256]{3,2,1,0:T(8,128)(2,1)} fusion(bf16[16,6,384,256]{2,3,1,0:T(8,128)(2,1)} %copy.35, pred[16,6]{1,0:T(8,128)(4,1)S(1)} %copy.31, bf16[384,16,256,1]{2,1,0,3:T(8,128)(2,1)S(1)} %bitcast.50), kind=kOutput, calls=%fused_computation.10 | convolution fusion | flops 4847566848 | bytes 34603104 | tf_op jit(solution)/shard_map/tjkc,tjd->jkcd/dot_general | solution.py:75
  623.2 2.4 copy.42
  625.6 2.8 convert_element_type.60
  628.4 36.7 %reduce-scatter.5.cloned.1.call-done = bf16[384,2048]{1,0:T(8,128)(2,1)} async-done(((bf16[384,8192]{1,0:T(8,128)(2,1)}), bf16[384,2048]{1,0:T(8,128)(2,1)}) %reduce-scatter.5.cloned.1.call-update) | async-done | bytes 1572880 | tf_op jit(solution)/shard_map/reduce_scatter | solution.py:92
  665.1 4.1 convert_add_fusion
  669.1 210.2 %reduce-scatter.7.cloned.1.call-done = bf16[16,6,64,256]{3,2,1,0:T(8,128)(2,1)} async-done(((bf16[16,6,256,256]{3,2,1,0:T(8,128)(2,1)}), bf16[16,6,64,256]{3,2,1,0:T(8,128)(2,1)}) %reduce-scatter.7.cloned.1.call-update) | async-done | bytes 3145744 | tf_op jit(solution)/shard_map/reduce_scatter | solution.py:78
  879.3 5.5 convert_element_type.55
  (57 shorter events, 7.5 us)
Async XLA Ops:
  7.2 2.8 copy-start.4
  7.2 53.7 %all-gather.5.cloned.1.call-start = ((), (), s32[]{:S(2)}) async-start(), calls=%async_computation.4 | async-start | bytes 7864320 | tf_op jit(solution)/shard_map/all_gather | solution.py:23
  9.9 109.3 %all-gather.9.cloned.1.call-start = ((), (), s32[]{:S(2)}) async-start(), calls=%async_computation.6 | async-start | bytes 10485760 | tf_op jit(solution)/shard_map/all_gather | solution.py:41
  9.9 17.0 %collective-permute-start = (bf16[2048,128]{1,0:T(8,128)(2,1)S(1)}, bf16[2048,128]{1,0:T(8,128)(2,1)S(1)}, u32[]{:S(2)}, u32[]{:S(2)}) collective-permute-start(bf16[2048,128]{1,0:T(8,128)(2,1)S(1)} %copy-done.4), channel_id=1, source_target_pairs={{0,4},{4,8},{8,12},{12,0},{1,5},{5,9},{9,13},{13,1},{2,6},{6,10},{... | collective-permute-start | bytes 1572872 | tf_op jit(solution)/shard_map/ppermute | solution.py:37
  27.0 14.9 %collective-permute-start.1 = (bf16[2048,128]{1,0:T(8,128)(2,1)S(1)}, bf16[2048,128]{1,0:T(8,128)(2,1)S(1)}, u32[]{:S(2)}, u32[]{:S(2)}) collective-permute-start(bf16[2048,128]{1,0:T(8,128)(2,1)S(1)} %collective-permute-done), channel_id=1, source_target_pairs={{0,4},{4,8},{8,12},{12,0},{1,5},{5,9},{9,13},{13,1},{2,6},{6,10},{... | collective-permute-start | bytes 1572872 | tf_op jit(solution)/shard_map/ppermute | solution.py:37
  41.9 14.0 %collective-permute-start.2 = (bf16[2048,128]{1,0:T(8,128)(2,1)S(1)}, bf16[2048,128]{1,0:T(8,128)(2,1)S(1)}, u32[]{:S(2)}, u32[]{:S(2)}) collective-permute-start(bf16[2048,128]{1,0:T(8,128)(2,1)S(1)} %collective-permute-done.1), channel_id=1, source_target_pairs={{0,4},{4,8},{8,12},{12,0},{1,5},{5,9},{9,13},{13,1},{2,6},{6,10},{... | collective-permute-start | bytes 1572872 | tf_op jit(solution)/shard_map/ppermute | solution.py:37
  58.9 1.6 copy-start.6
  58.9 280.0 %all-gather.7.cloned.1.call-start = ((), (), s32[]{:S(2)}) async-start(), calls=%async_computation.5 | async-start | bytes 15728640 | tf_op jit(solution)/shard_map/all_gather | solution.py:32
  59.7 359.7 %all-gather.11.cloned.1.call-start = ((), (), s32[]{:S(2)}) async-start(), calls=%async_computation.7 | async-start | bytes 5242880 | tf_op jit(solution)/shard_map/all_gather | solution.py:48
  60.2 403.6 %all-reduce.2.cloned.1.call-start = ((), (), s32[]{:S(2)}) async-start(), calls=%async_computation.9 | async-start | bytes 786432 | tf_op jit(solution)/shard_map/psum | solution.py:61
  419.4 10.5 %copy-start.7 = (bf16[512,4096]{1,0:T(8,128)(2,1)S(1)}, bf16[512,4096]{1,0:T(8,128)(2,1)}, u32[]{:S(2)}) copy-start(bf16[512,4096]{1,0:T(8,128)(2,1)} %all-gather.11.cloned.1.call-done) | copy-start | bytes 12582916
  429.9 38.2 %copy-start.3 = (bf16[384,4096]{1,0:T(8,128)(2,1)}, bf16[384,4096]{1,0:T(8,128)(2,1)S(1)}, u32[]{:S(2)}) copy-start(bf16[384,4096]{1,0:T(8,128)(2,1)S(1)} %get-tuple-element.22) | copy-start | bytes 9437188
  432.5 190.7 %reduce-scatter.9.cloned.1.call-start = ((), (), s32[]{:S(2)}) async-start(), calls=%async_computation.11 | async-start | bytes 2621440 | tf_op jit(solution)/shard_map/reduce_scatter | solution.py:71
  468.0 157.6 %reduce-scatter.11.cloned.1.call-start = ((), (), s32[]{:S(2)}) async-start(), calls=%async_computation.12 | async-start | bytes 5242880 | tf_op jit(solution)/shard_map/reduce_scatter | solution.py:65
  472.5 192.6 %reduce-scatter.5.cloned.1.call-start = ((), (), s32[]{:S(2)}) async-start(), calls=%async_computation.8 | async-start | bytes 7864320 | tf_op jit(solution)/shard_map/reduce_scatter | solution.py:92
  476.0 25.3 %copy-start.1 = (bf16[48,8,16,256]{3,2,1,0:T(8,128)(2,1)}, bf16[48,8,16,256]{3,2,1,0:T(8,128)(2,1)S(1)}, u32[]{:S(2)}) copy-start(bf16[48,8,16,256]{3,2,1,0:T(8,128)(2,1)S(1)} %copy.52) | copy-start | bytes 9437188
  606.5 1.9 copy-start.2
  606.5 272.8 %reduce-scatter.7.cloned.1.call-start = ((), (), s32[]{:S(2)}) async-start(), calls=%async_computation.10 | async-start | bytes 15728640 | tf_op jit(solution)/shard_map/reduce_scatter | solution.py:78
  623.2 41.9 %copy-start = (bf16[2048,512]{1,0:T(8,128)(2,1)S(1)}, bf16[2048,512]{1,0:T(8,128)(2,1)}, u32[]{:S(2)}) copy-start(bf16[2048,512]{1,0:T(8,128)(2,1)} %constant_dynamic-slice_fusion) | copy-start | bytes 6291460
  623.2 41.9 %copy-start.5 = (bf16[384,512]{1,0:T(8,128)(2,1)S(1)}, bf16[384,512]{1,0:T(8,128)(2,1)}, u32[]{:S(2)}) copy-start(bf16[384,512]{1,0:T(8,128)(2,1)} %all-reduce.2.cloned.1.call-done) | copy-start | bytes 1179652
Sparse Core Ops, SparseCore 0:
  10.1 49.0 all-gather.4
  60.8 58.2 all-gather.8
  120.7 218.2 all-gather.6
  340.4 78.9 all-gather.10
  432.6 31.1 all-reduce.1
  468.1 43.8 reduce-scatter.8
  514.3 76.0 reduce-scatter.10
  606.6 58.3 reduce-scatter.4
  667.4 211.8 reduce-scatter.6
